TPU v7x, 128 devices: a whole 4x4x4 slice. The times are simulated.
128 devices in a mesh: grp: 4 (over x_hi, core), dp: 32 (over z, x_lo, y).
Axes of the slice: x: 4 (x_hi: 2, x_lo: 2; x = x_hi * 2 + x_lo), y: 4, z: 4, core: 2. Of those that a mesh axis runs over, the one named last changes fastest.
Arguments:
- normed: bfloat16 [65536, 1280], P(('grp', 'dp')), may hold values from -6 to 6
- w_in: bfloat16 [5120, 1280], replicated, may hold values from -0.15625 to 0.15625
- w_out: bfloat16 [1280, 2560], replicated, may hold values from -0.125 to 0.125
- cotangent: bfloat16 [65536, 1280], P(('grp', 'dp')), may hold values from -24 to 24
Outputs:
- grad_in: float32 [5120, 1280], P('dp')
- grad_out: float32 [1280, 2560], P('dp')
- grad_normed: bfloat16 [65536, 1280], P(('grp', 'dp'))
All inputs are finite; a program needn't handle non-finite values.
Results may differ from a plain program's by a relative error of at most 0.005.
Values sent between devices are 32-bit elements; how exact they have to be, the bound alone decides.
No kernel may reach another device: no remote copies, remote signals or barrier semaphores. Data moves between devices by JAX's collectives and lax.ppermute only.
A program may use at most 192 MiB of HBM per device.

v0:
```python
import jax
import jax.numpy as jnp
from jax import lax
from jax.sharding import PartitionSpec as P


def cross_dot(left, right):
    return lax.dot_general(
        left, right, (((0,), (0,)), ((), ())), preferred_element_type=jnp.float32
    )


def local(normed, w_in, w_out, cotangent):
    width = w_out.shape[1]
    inner = lax.axis_size("dp")
    outer = lax.axis_size("grp")
    factor = (normed.shape[0] * inner * outer) ** (-0.5)
    proj = lax.dot_general(
        normed, w_in, (((1,), (1,)), ((), ())), preferred_element_type=jnp.float32
    )
    value = proj[:, :width]
    gate = proj[:, width:]
    cdf = 0.5 * (1.0 + lax.erf(gate * 2.0 ** (-0.5)))
    density = jnp.exp(-0.5 * gate * gate) * (2.0 * jnp.pi) ** (-0.5)
    act = (value * gate * cdf).astype(jnp.bfloat16)
    dact = jnp.dot(cotangent, w_out, preferred_element_type=jnp.float32)
    d_value = dact * gate * cdf
    d_gate = dact * value * (cdf + gate * density)
    dproj = jnp.concatenate([d_value, d_gate], axis=1).astype(jnp.bfloat16)
    grad_normed = jnp.dot(dproj, w_in, preferred_element_type=jnp.float32).astype(jnp.bfloat16)
    columns = dproj
    piece_in = lax.psum_scatter(
        cross_dot(columns, normed) * factor, "dp", scatter_dimension=0, tiled=True
    )
    columns = cotangent
    piece_out = lax.psum_scatter(
        cross_dot(columns, act) * factor, "dp", scatter_dimension=0, tiled=True
    )
    grad_in, grad_out = lax.psum((piece_in, piece_out), "grp")
    return (grad_in, grad_out, grad_normed)


def solution(mesh):
    placed = (P(("grp", "dp"), None), P(), P(), P(("grp", "dp"), None))
    return jax.shard_map(
        local,
        mesh=mesh,
        in_specs=placed,
        out_specs=(P("dp", None), P("dp", None), P(("grp", "dp"), None)),
        check_vma=False,
    )
```

profile of v0, /device:TPU:1, one launch (start us, length us, event | category | flops | bytes accessed | tf_op | source)
XLA Modules:
  0.0 596.3 jit_solution(10234275133338313674)
XLA Ops:
  7.2 0.0 copy-start
  7.2 0.0 copy-start.2
  7.2 0.0 reduce-scatter.7.cloned.1.call-start
  7.2 1.3 copy-done
  8.5 12.4 %fusion.11 = f32[512,5120]{1,0:T(8,128)} fusion(bf16[512,1280]{1,0:T(8,128)(2,1)S(1)} %copy-done, bf16[5120,1280]{1,0:T(8,128)(2,1)} %param.5), kind=kOutput, calls=%fused_computation.18 | convolution fusion | flops 6710886400 | bytes 24903680 | tf_op jit(solution)/shard_map/dot_general | solution.py:18
  20.9 0.0 copy-done.2
  20.9 9.2 %fusion = f32[1280,2560]{0,1:T(8,128)} fusion(bf16[512,1280]{1,0:T(8,128)(2,1)S(1)} %copy-done.2, f32[512,5120]{1,0:T(8,128)} %fusion.11), kind=kOutput, calls=%fused_computation.2 | convolution fusion | flops 3366584320 | bytes 24903680 | tf_op jit(solution)/shard_map/dot_general | solution.py:8
  30.0 13.9 %copy.9 = f32[1280,2560]{1,0:T(8,128)} copy(f32[1280,2560]{0,1:T(8,128)} %fusion) | data formatting | bytes 26214400
  43.9 0.0 reduce-scatter.7.cloned.1.call-update
  44.0 0.0 reduce-scatter.5.cloned.1.call-start
  44.0 8.6 %multiply_convert_fusion.1 = (bf16[512,2560]{1,0:T(8,128)(2,1)S(1)}, bf16[512,2560]{1,0:T(8,128)(2,1)S(1)}) fusion(f32[512,5120]{1,0:T(8,128)} %fusion.11, bf16[512,1280]{1,0:T(8,128)(2,1)S(1)} %copy-done.2, bf16[1280,2560]{1,0:T(8,128)(2,1)} %param.6), kind=kOutput, calls=%fused_computation.12 | convolution fusion | flops 3373793280 | bytes 23592960 | tf_op jit(solution)/shard_map/dot_general | solution.py:26
  52.6 0.0 copy-start.3
  52.7 0.0 copy-start.4
  52.7 1.5 copy-done.3
  54.2 0.8 copy-done.4
  55.0 12.4 %convolution_multiply_fusion = f32[5120,1280]{1,0:T(8,128)} fusion(bf16[512,1280]{1,0:T(8,128)(2,1)S(1)} %copy-done, bf16[512,2560]{1,0:T(8,128)(2,1)S(1)} %get-tuple-element.12, bf16[512,2560]{1,0:T(8,128)(2,1)S(1)} %get-tuple-element.11), kind=kOutput, calls=%fused_computation | convolution fusion | flops 6727925760 | bytes 32768000 | tf_op jit(solution)/shard_map/dot_general | solution.py:8
  67.4 0.0 reduce-scatter.5.cloned.1.call-update
  67.4 0.2 all-reduce.3.cloned.1.call-start
  67.6 148.6 %reduce-scatter.7.cloned.1.call-done = f32[40,2560]{1,0:T(8,128)} async-done(((f32[1280,2560]{1,0:T(8,128)}), f32[40,2560]{1,0:T(8,128)}) %reduce-scatter.7.cloned.1.call-update) | async-done | bytes 409616
  216.2 2.5 copy.10
  218.7 307.4 %reduce-scatter.5.cloned.1.call-done = f32[160,1280]{1,0:T(8,128)} async-done(((f32[5120,1280]{1,0:T(8,128)}), f32[160,1280]{1,0:T(8,128)}) %reduce-scatter.5.cloned.1.call-update) | async-done | bytes 819216 | tf_op jit(solution)/shard_map/reduce_scatter | solution.py:32
  526.1 0.0 all-reduce.3.cloned.1.call-update
  526.1 0.0 copy-start.1
  526.2 13.6 %fusion.8 = bf16[512,1280]{1,0:T(8,128)(2,1)} fusion(bf16[5120,1280]{1,0:T(8,128)(2,1)} %param.5, bf16[512,2560]{1,0:T(8,128)(2,1)} %copy-done.4, bf16[512,2560]{1,0:T(8,128)(2,1)} %copy-done.3), kind=kOutput, calls=%fused_computation.15 | convolution fusion | flops 6722027520 | bytes 19660800 | tf_op jit(solution)/shard_map/dot_general | solution.py:30
  539.7 45.5 %all-reduce.3.cloned.1.call-done = (f32[160,1280]{1,0:T(8,128)}, f32[40,2560]{0,1:T(8,128)}) async-done(((f32[160,1280]{1,0:T(8,128)}, f32[40,2560]{0,1:T(8,128)}), (f32[160,1280]{1,0:T(8,128)}, f32[40,2560]{0,1:T(8,128)})) %all-reduce.3.cloned.1.call-update) | async-done | bytes 1228816 | tf_op jit(solution)/shard_map/psum | solution.py:39
  585.2 2.4 copy.8
  587.7 2.1 copy.13
  589.7 0.0 copy-done.1
Async XLA Ops:
  7.2 1.3 copy-start
  7.2 13.7 %copy-start.2 = (bf16[512,1280]{1,0:T(8,128)(2,1)S(1)}, bf16[512,1280]{1,0:T(8,128)(2,1)}, u32[]{:S(2)}) copy-start(bf16[512,1280]{1,0:T(8,128)(2,1)} %param.7) | copy-start | bytes 3932164
  7.2 209.0 %reduce-scatter.7.cloned.1.call-start = ((), (), s32[]{:S(2)}) async-start(), calls=%async_computation.3 | async-start | bytes 13516800
  44.0 482.2 %reduce-scatter.5.cloned.1.call-start = ((), (), s32[]{:S(2)}) async-start(), calls=%async_computation.2 | async-start | bytes 27033600 | tf_op jit(solution)/shard_map/reduce_scatter | solution.py:32
  52.6 1.5 copy-start.3
  52.7 2.3 copy-start.4
  67.4 517.8 %all-reduce.3.cloned.1.call-start = ((), (), s32[]{:S(2)}) async-start(), calls=%async_computation.4 | async-start | bytes 4259840 | tf_op jit(solution)/shard_map/psum | solution.py:39
  526.1 63.6 %copy-start.1 = (bf16[512,1280]{1,0:T(8,128)(2,1)S(1)}, bf16[512,1280]{1,0:T(8,128)(2,1)}, u32[]{:S(2)}) copy-start(bf16[512,1280]{1,0:T(8,128)(2,1)} %param.4) | copy-start | bytes 3932164
Sparse Core Ops, SparseCore 0:
  44.1 172.0 reduce-scatter.6
  218.8 307.2 reduce-scatter.4
  528.9 56.2 all-reduce.2
where the time goes:
time: 597 us; the launch traced here: 596 us
  waiting for transfers between devices  502 us (84%)
  matrix products  56.2 us (9%)
  local copies, waits for them, and re-layouts  24.5 us (4%)
  between operations  13.8 us (2%)
    reduce_scatter x1, waiting for transfers between devices, local(): lax.psum_scatter(cross_dot(columns, normed) * factor, 'dp', scatter_dimen...  307 us
    unnamed x4, waiting for transfers between devices  149 us
    psum x1, waiting for transfers between devices, local(): grad_in, grad_out = lax.psum((piece_in, piece_out), 'grp')  45.5 us
    unnamed x14, local copies, waits for them, and re-layouts  24.5 us
    dot_general x2, matrix products, cross_dot(): lax.dot_general(left, right, (((0,), (0,)), ((), ())), preferred_element_...  21.6 us
    dot_general x1, matrix products, local(): jnp.dot(dproj, w_in, preferred_element_type=jnp.float32)  13.6 us
    dot_general x1, matrix products, local(): lax.dot_general(normed, w_in, (((1,), (1,)), ((), ())), preferred_element...  12.4 us
  transfers between devices with their start and end apart: 3, of which 3 were waited for; matrix products, arithmetic and copies ran while one was open for 6% of the time, Pallas kernels for 0%

commit v1 on v0

v1 whole, which is shorter than its diff:
```python
import functools

import jax
import jax.numpy as jnp
from jax import lax
from jax.experimental import pallas as pl
from jax.experimental.pallas import tpu as pltpu
from jax.sharding import PartitionSpec as P

AXES = ("grp", "dp")
BF = jnp.bfloat16
F32 = jnp.float32
VMEM_LIMIT = 56 * 1024 * 1024


def place(x, y, z, c):
    return ((x // 2) * 2 + c) * 32 + z * 8 + (x % 2) * 4 + y


EVERY = [(x, y, z, c) for x in range(4) for y in range(4) for z in range(4) for c in range(2)]


def halving_pairs(axis, step):
    pairs = []
    for x, y, z, c in EVERY:
        at = [x, y, z]
        phase = (c + step) % 2
        at[axis] = (at[axis] + (1 if at[axis] % 2 == phase else -1)) % 4
        pairs.append((place(x, y, z, c), place(*at, c)))
    return pairs


CORE_PAIRS = [(place(x, y, z, c), place(x, y, z, 1 - c)) for x, y, z, c in EVERY]
FAR_PAIRS = [(place(x, y, z, c), place((x + 2) % 4, y, z, c)) for x, y, z, c in EVERY]


def owner_pairs(shift):
    return [
        (place((x + shift) % 4, y, z, c), place(x, y, z, c))
        for x, y, z, c in EVERY
        if x % 2 == c
    ]


def halves(at, core):
    keep0 = jnp.where(core == 0, jnp.where((at == 1) | (at == 2), 1, 0), jnp.where(at >= 2, 2, 0))
    keep1 = jnp.where(core == 0, 3 - keep0, keep0 + 1)
    send0 = jnp.where(core == 0, 1 - keep0, 2 - keep0)
    send1 = jnp.where(core == 0, 3 - send0, send0 + 1)
    own = jnp.where(core == 0, at // 2, at % 2)
    return (keep0, keep1), (send0, send1), own


def terms_kernel(core_ref, normed_ref, cot_ref, win_ref, wout_ref, dproj_ref, dproj_t_ref, act_ref, cot_t_ref):
    width = wout_ref.shape[1]
    normed = normed_ref[...].astype(BF)
    cot = cot_ref[...].astype(BF)
    w = win_ref[...].reshape(2 * width, win_ref.shape[-1])
    proj = lax.dot_general(normed, w, (((1,), (1,)), ((), ())), preferred_element_type=F32)
    dact = jnp.dot(cot, wout_ref[...], preferred_element_type=F32)
    value = proj[:, :width]
    gate = proj[:, width:]
    cdf = 0.5 * (1.0 + lax.erf(gate * (2.0 ** -0.5)))
    density = jnp.exp(-0.5 * gate * gate) * ((2.0 * jnp.pi) ** -0.5)
    gated = gate * cdf
    act_ref[0] = (value * gated).astype(BF)
    d_value = (dact * gated).astype(BF)
    d_gate = (dact * value * (cdf + gate * density)).astype(BF)
    dproj_ref[0, :, :width] = d_value
    dproj_ref[0, :, width:] = d_gate
    dproj_t_ref[0, 0] = d_value.T
    dproj_t_ref[0, 1] = d_gate.T

    @pl.when(pl.program_id(0) == 0)
    def _():
        cot_t_ref[...] = cot.T


def terms(core, normed, cot, win, wout, tile=256):
    tokens, dim = normed.shape
    width = win.shape[3]
    steps = tokens // tile
    last = steps - 1
    return pl.pallas_call(
        terms_kernel,
        grid_spec=pltpu.PrefetchScalarGridSpec(
            num_scalar_prefetch=1,
            grid=(2, steps),
            in_specs=[
                pl.BlockSpec((tile, dim), lambda k, t, c: (t, 0)),
                pl.BlockSpec((tile, dim), lambda k, t, c: (t, 0)),
                pl.BlockSpec((2, None, None, width, dim), lambda k, t, c: (0, k, c[0], 0, 0)),
                pl.BlockSpec((dim, width), lambda k, t, c: (0, k * 2 + c[0])),
            ],
            out_specs=[
                pl.BlockSpec((1, tile, 2 * width), lambda k, t, c: (k, t, 0)),
                pl.BlockSpec((1, 2, width, tile), lambda k, t, c: (k, 0, 0, t)),
                pl.BlockSpec((1, tile, width), lambda k, t, c: (k, t, 0)),
                pl.BlockSpec((dim, tile), lambda k, t, c: (0, jnp.where(k == 0, t, last))),
            ],
        ),
        out_shape=[
            jax.ShapeDtypeStruct((2, tokens, 2 * width), BF),
            jax.ShapeDtypeStruct((2, 2, width, tokens), BF),
            jax.ShapeDtypeStruct((2, tokens, width), BF),
            jax.ShapeDtypeStruct((dim, tokens), BF),
        ],
        compiler_params=pltpu.CompilerParams(vmem_limit_bytes=VMEM_LIMIT),
        cost_estimate=pl.CostEstimate(
            flops=2 * tokens * dim * width * 6, bytes_accessed=20 * 2**20, transcendentals=0
        ),
        name="terms",
    )(core, normed, cot, win, wout)


def grad_in_kernel(
    tab, d_own, d_oth, n_own, n_oth, a_send, a_keep, b_send, b_keep, a_buf, b_buf, n_bf, sems
):
    half = a_buf.shape[-1]
    block = b_buf.shape[2]
    n_bf[...] = n_oth[...].astype(BF)
    kept = tab[0]
    copies = []
    for slot, (which, out) in enumerate(((1 - kept, a_send), (kept, a_keep))):
        a_buf[slot] = jnp.dot(
            d_own[which], n_own[:, :half], preferred_element_type=F32
        ) + jnp.dot(d_oth[which], n_bf[:, :half], preferred_element_type=F32)
        copy = pltpu.make_async_copy(a_buf.at[slot], out, sems.at[slot])
        copy.start()
        copies.append(copy)
    at = 2
    for which in range(2):
        total = jnp.dot(d_own[which], n_own[:, half:], preferred_element_type=F32) + jnp.dot(
            d_oth[which], n_bf[:, half:], preferred_element_type=F32
        )
        b_buf[which] = total.reshape(4, block, half)
        for i, (quarter, out) in enumerate(
            ((tab[3], b_send), (tab[4], b_send), (tab[1], b_keep), (tab[2], b_keep))
        ):
            copy = pltpu.make_async_copy(b_buf.at[which, quarter], out.at[which, i % 2], sems.at[at])
            at += 1
            copy.start()
            copies.append(copy)
    for copy in copies:
        copy.wait()


def grad_in_chunk(tab, d_own, d_oth, n_own, n_oth, chunk):
    tokens, dim = n_own.shape
    width = d_own.shape[2]
    half = dim // 2
    block = width // 4
    one = jax.ShapeDtypeStruct((width, half), F32)
    two = jax.ShapeDtypeStruct((2, 2, block, half), F32)
    d_spec = pl.BlockSpec((None, 2, width, tokens), lambda i, t: (chunk, 0, 0, 0))
    n_spec = pl.BlockSpec((tokens, dim), lambda i, t: (0, 0))
    return pl.pallas_call(
        grad_in_kernel,
        grid_spec=pltpu.PrefetchScalarGridSpec(
            num_scalar_prefetch=1,
            grid=(1,),
            in_specs=[d_spec, d_spec, n_spec, n_spec],
            out_specs=[pl.BlockSpec(memory_space=pl.ANY)] * 4,
            scratch_shapes=[
                pltpu.VMEM((2, width, half), F32),
                pltpu.VMEM((2, 4, block, half), F32),
                pltpu.VMEM((tokens, dim), BF),
                pltpu.SemaphoreType.DMA((10,)),
            ],
        ),
        out_shape=[one, one, two, two],
        compiler_params=pltpu.CompilerParams(vmem_limit_bytes=VMEM_LIMIT),
        cost_estimate=pl.CostEstimate(
            flops=2 * 2 * tokens * dim * width * 2, bytes_accessed=12 * 2**20, transcendentals=0
        ),
        name="grad_in_chunk",
    )(tab, d_own, d_oth, n_own, n_oth)


def grad_out_kernel(tab, c_own, c_oth, act_own, act_oth, send, keep, buf, sems):
    total = jnp.dot(c_own[...], act_own[...], preferred_element_type=F32) + jnp.dot(
        c_oth[...], act_oth[...], preferred_element_type=F32
    )
    buf[...] = total.reshape(buf.shape)
    kept = tab[0]
    copies = []
    for i in range(4):
        copies.append(pltpu.make_async_copy(buf.at[i, 1 - kept], send.at[i], sems.at[0, i]))
        copies.append(pltpu.make_async_copy(buf.at[i, kept], keep.at[i], sems.at[1, i]))
    for copy in copies:
        copy.start()
    for copy in copies:
        copy.wait()


def grad_out_chunk(tab, c_own, c_oth, act_own, act_oth, chunk):
    dim, tokens = c_own.shape
    width = act_own.shape[2]
    block = dim // 8
    one = jax.ShapeDtypeStruct((4, block, width), F32)
    c_spec = pl.BlockSpec((dim, tokens), lambda i, t: (0, 0))
    a_spec = pl.BlockSpec((None, tokens, width), lambda i, t: (chunk, 0, 0))
    return pl.pallas_call(
        grad_out_kernel,
        grid_spec=pltpu.PrefetchScalarGridSpec(
            num_scalar_prefetch=1,
            grid=(1,),
            in_specs=[c_spec, c_spec, a_spec, a_spec],
            out_specs=[pl.BlockSpec(memory_space=pl.ANY)] * 2,
            scratch_shapes=[
                pltpu.VMEM((4, 2, block, width), F32),
                pltpu.SemaphoreType.DMA((2, 4)),
            ],
        ),
        out_shape=[one, one],
        compiler_params=pltpu.CompilerParams(vmem_limit_bytes=VMEM_LIMIT),
        cost_estimate=pl.CostEstimate(
            flops=2 * 2 * tokens * dim * width, bytes_accessed=8 * 2**20, transcendentals=0
        ),
        name="grad_out_chunk",
    )(tab, c_own, c_oth, act_own, act_oth)


def back_kernel(core_ref, d_ref, w_ref, *rest):
    rest, total = rest[:-1], rest[-1]
    out = rest[-1]
    w = w_ref[...].reshape(2 * w_ref.shape[1], w_ref.shape[2])
    part = jnp.dot(d_ref[...], w, preferred_element_type=F32)

    @pl.when(pl.program_id(0) == 0)
    def _():
        total[...] = part

    @pl.when(pl.program_id(0) == 1)
    def _():
        whole = total[...] + part
        if len(rest) > 1:
            whole = whole + rest[0][...]
        out[...] = whole.astype(out.dtype)


def back(core, dproj, win, dtype, *more):
    _, tokens, both = dproj.shape
    width, dim = win.shape[3:]
    whole = pl.BlockSpec((tokens, dim), lambda k, c: (0, 0))
    return pl.pallas_call(
        back_kernel,
        grid_spec=pltpu.PrefetchScalarGridSpec(
            num_scalar_prefetch=1,
            grid=(2,),
            in_specs=[
                pl.BlockSpec((None, tokens, both), lambda k, c: (k, 0, 0)),
                pl.BlockSpec((2, None, None, width, dim), lambda k, c: (0, k, c[0], 0, 0)),
            ]
            + [whole] * len(more),
            out_specs=whole,
            scratch_shapes=[pltpu.VMEM((tokens, dim), F32)],
        ),
        out_shape=jax.ShapeDtypeStruct((tokens, dim), dtype),
        compiler_params=pltpu.CompilerParams(vmem_limit_bytes=VMEM_LIMIT),
        cost_estimate=pl.CostEstimate(
            flops=2 * tokens * dim * both * 2, bytes_accessed=12 * 2**20, transcendentals=0
        ),
        name="back",
    )(core, dproj, win, *more)


def move(array, pairs):
    return lax.ppermute(array, AXES, pairs)


def pick(array, axis, index):
    return lax.dynamic_index_in_dim(array, index, axis, keepdims=False)


def pick_two(array, axis, indices):
    return jnp.concatenate([lax.dynamic_slice_in_dim(array, i, 1, axis) for i in indices], axis)


def halve(array, axis_at, mesh_axis, at, core):
    keep, send, own = halves(at, core)
    got = move(pick_two(array, axis_at, send), halving_pairs(mesh_axis, 0))
    array = pick_two(array, axis_at, keep) + got
    return finish(array, axis_at, mesh_axis, own)


def finish(array, axis_at, mesh_axis, own):
    got = move(pick(array, axis_at, 1 - own), halving_pairs(mesh_axis, 1))
    return pick(array, axis_at, own) + got


def local(normed, w_in, w_out, cotangent):
    dim = normed.shape[1]
    width = w_out.shape[1] // 4
    factor = (normed.shape[0] * lax.axis_size("dp") * lax.axis_size("grp")) ** (-0.5)
    grp, dp = lax.axis_index("grp"), lax.axis_index("dp")
    core = grp % 2
    z, x, y = dp // 8, (grp // 2) * 2 + (dp % 8) // 4, dp % 4
    win = w_in.reshape(2, 2, 2, width, dim)
    core_1 = core.reshape(1).astype(jnp.int32)

    wide = lax.optimization_barrier((normed.astype(F32), cotangent.astype(F32)))
    n_oth = move(wide[0], CORE_PAIRS)
    c_oth = move(wide[1], CORE_PAIRS)
    d_own, dt_own, act_own, ct_own = terms(core_1, normed, cotangent, win, w_out)
    d_oth, dt_oth, act_oth, ct_oth = terms(core_1, n_oth, c_oth, win, w_out)

    keep_z, _, own_z = halves(z, core)
    keep_x, _, own_x = halves(x, core)
    keep_y, send_y, own_y = halves(y, core)
    own_z_chunk = z % 2
    own_x_chunk = jnp.where(core == 0, x // 2, (x // 2) ^ (x % 2))

    a, b, c = [], [], []
    for chunk in range(2):
        kept_gate = jnp.where(core == 0, keep_z[0] ^ chunk, keep_z[0] // 2)
        tab = jnp.stack([kept_gate, *keep_y, *send_y]).astype(jnp.int32)
        kept_x = jnp.where(core == 0, keep_x[0] ^ chunk, (keep_x[0] // 2) ^ chunk)
        c_send, c_keep = grad_out_chunk(
            kept_x.reshape(1).astype(jnp.int32), ct_own, ct_oth, act_own, act_oth, chunk
        )
        a_send, a_keep, b_send, b_keep = grad_in_chunk(tab, dt_own, dt_oth, normed, n_oth, chunk)
        c.append(c_keep + move(c_send, halving_pairs(0, 0)))
        a.append(a_keep + move(a_send, halving_pairs(2, 0)))
        b.append(b_keep + move(b_send, halving_pairs(1, 0)))

    back_oth = back(core_1, d_oth, win, F32)
    grad_normed = back(core_1, d_own, win, BF, move(back_oth, CORE_PAIRS))

    half = dim // 2
    a = finish(jnp.stack(a), 0, 2, own_z_chunk).reshape(4, 4, width // 16, half)
    b = finish(jnp.stack(b), 2, 1, own_y).reshape(2, 2, 4, width // 16, half)
    c = finish(jnp.stack(c), 0, 0, own_x_chunk).reshape(4, 4, dim // 32, width)

    a = halve(a, 0, 1, y, core)
    b = halve(b, 2, 0, x, core)
    c = halve(c, 0, 2, z, core)
    b = b.transpose(1, 0, 2, 3).reshape(4, width // 16, half)

    a = halve(a, 0, 0, x, core)
    b = halve(b, 0, 2, z, core)
    c = halve(c, 0, 1, y, core)

    piece_in = jnp.concatenate([a, b], axis=1) * factor
    piece_out = c * factor
    far_out = move(piece_out, FAR_PAIRS)
    mine_in = [piece_in] + [move(piece_in, owner_pairs(s)) for s in (1, 2, 3)]
    stacked = jnp.stack(mine_in + mine_in)
    rows_in = lax.dynamic_slice_in_dim(stacked, (4 - x) % 4, 4, 0).reshape(width // 4, dim)
    pair_out = jnp.stack([piece_out, far_out, piece_out])
    rows_out = lax.dynamic_slice_in_dim(pair_out, own_x_chunk, 2, 0)

    other_in = move(rows_in, CORE_PAIRS)
    other_out = move(rows_out, CORE_PAIRS)
    grad_in = jnp.where(x % 2 == core, rows_in, other_in)
    first = jnp.where(core == 0, rows_out, other_out)
    second = jnp.where(core == 0, other_out, rows_out)
    grad_out = jnp.concatenate([first[0], second[0], first[1], second[1]], axis=1)
    return (grad_in, grad_out, grad_normed)


def solution(mesh):
    placed = (P(AXES, None), P(), P(), P(AXES, None))
    return jax.shard_map(
        local,
        mesh=mesh,
        in_specs=placed,
        out_specs=(P("dp", None), P("dp", None), P(AXES, None)),
        check_vma=False,
    )
```

time: 597 us -> 216 us (0.36)
  waiting for transfers between devices: 502 us -> 64.3 us
  Pallas kernels: 0 us -> 75.7 us
  matrix products: 56.2 us -> 0 us
  starting transfers between devices: 0.3 us -> 42.7 us
  other arithmetic: 0 us -> 23 us
  local copies, waits for them, and re-layouts: 24.5 us -> 8.15 us
  between operations: 13.8 us -> 1.32 us
    reduce_scatter x1 -> x0, waiting for transfers between devices: 307 us -> none  [local(): lax.psum_scatter(cross_dot(columns, normed) * factor, 'dp', scatter_dimen...]
    unnamed x4 -> x0, waiting for transfers between devices: 149 us -> none
    pallas_call x0 -> x8, Pallas kernels: none -> 75.7 us  [the longest x2 28.8 us: terms(): pl.pallas_call(terms_kernel, grid_spec=pltpu.PrefetchScalarGridSpec(num_s...]
    ppermute x0 -> x30, waiting for transfers between devices: none -> 64.3 us  [move(): return lax.ppermute(array, AXES, pairs)]
    dot_general x5 -> x0, matrix products: 56.2 us -> none  [the longest x2 21.6 us: cross_dot(): lax.dot_general(left, right, (((0,), (0,)), ((), ())), preferred_element_...]
    psum x1 -> x0, waiting for transfers between devices: 45.5 us -> none  [local(): grad_in, grad_out = lax.psum((piece_in, piece_out), 'grp')]
    ppermute x0 -> x30, starting transfers between devices: none -> 42.7 us  [move(): return lax.ppermute(array, AXES, pairs)]
    unnamed x14 -> x37, local copies, waits for them, and re-layouts: 24.5 us -> 5.95 us
  transfers between devices with their start and end apart: 3 -> 30, of which waited for: 3 -> 12; matrix products, arithmetic and copies ran while one was open for 6% -> 9% of each run, Pallas kernels for 0% -> 25%
where the time goes in v1:
time: 216 us; the launch traced here: 215 us
  Pallas kernels  75.7 us (35%)
  waiting for transfers between devices  64.3 us (30%)
  starting transfers between devices  42.7 us (20%)
  other arithmetic  23 us (11%)
  local copies, waits for them, and re-layouts  8.15 us (4%)
    ppermute x30, waiting for transfers between devices, move(): return lax.ppermute(array, AXES, pairs)  64.3 us
    ppermute x30, starting transfers between devices, move(): return lax.ppermute(array, AXES, pairs)  42.7 us
    pallas_call x2, Pallas kernels, terms(): pl.pallas_call(terms_kernel, grid_spec=pltpu.PrefetchScalarGridSpec(num_s...  28.8 us
    pallas_call x2, Pallas kernels, grad_in_chunk(): pl.pallas_call(grad_in_kernel, grid_spec=pltpu.PrefetchScalarGridSpec(num...  18.3 us
    pallas_call x2, Pallas kernels, back(): pl.pallas_call(back_kernel, grid_spec=pltpu.PrefetchScalarGridSpec(num_sc...  16.4 us
    pallas_call x2, Pallas kernels, grad_out_chunk(): pl.pallas_call(grad_out_kernel, grid_spec=pltpu.PrefetchScalarGridSpec(nu...  12.1 us
    unnamed x37, local copies, waits for them, and re-layouts  5.95 us
    add x7, other arithmetic, finish(): return pick(array, axis_at, own) + got  5.69 us
  transfers between devices with their start and end apart: 30, of which 12 were waited for; matrix products, arithmetic and copies ran while one was open for 9% of the time, Pallas kernels for 25%

profile of v1, /device:TPU:1, one launch (start us, length us, event | category | flops | bytes accessed | tf_op | source)
XLA Modules:
  0.0 215.2 jit_solution(10840984519756165305)
XLA Ops:
  0.6 3.2 %convert_element_type.7 = f32[512,1280]{1,0:T(8,128)} convert(bf16[512,1280]{1,0:T(8,128)(2,1)} %cot_ref.1) | non-fusion elementwise | flops 655360 | bytes 3932160 | tf_op jit(solution)/shard_map/convert_element_type | solution.py:302
  3.8 1.7 convert_element_type.6
  5.6 1.4 collective-permute-start
  7.0 14.0 %terms.2 = (bf16[2,512,1280]{2,1,0:T(8,128)(2,1)}, bf16[2,2,640,512]{3,2,1,0:T(8,128)(2,1)}, bf16[2,512,640]{2,1,0:T(8,128)(2,1)}, bf16[1280,512]{1,0:T(8,128)(2,1)}) custom-call(s32[1]{0:T(128)} %bitcast.5.core_ref, bf16[512,1280]{1,0:T(8,128)(2,1)} %n_own.3, bf16[512,1280]{1,0:T(8,128)(2,1)} %cot_ref.1, bf16[2,2,2,640,1280]{4,3,2,1,0:T(8,128)(2,1)} %bitcast.97, ...), custom_call_target="tpu_custom_call" | custom-call | flops 5033164800 | bytes 20971520 | tf_op jit(solution)/shard_map/terms/pallas_call | solution.py:84
  21.1 1.5 copy-done.8
  22.6 14.8 %terms.3 = (bf16[2,512,1280]{2,1,0:T(8,128)(2,1)}, bf16[2,2,640,512]{3,2,1,0:T(8,128)(2,1)}, bf16[2,512,640]{2,1,0:T(8,128)(2,1)}, bf16[1280,512]{1,0:T(8,128)(2,1)}) custom-call(s32[1]{0:T(128)} %bitcast.5.core_ref, f32[512,1280]{1,0:T(8,128)} %copy-done.8, f32[512,1280]{1,0:T(8,128)} %collective-permute-done.1.cot_ref, ...), custom_call_target="tpu_custom_call" | custom-call | flops 5033164800 | bytes 20971520 | tf_op jit(solution)/shard_map/terms/pallas_call | solution.py:84
  37.4 6.0 %grad_out_chunk.3 = (f32[4,160,640]{2,1,0:T(8,128)}, f32[4,160,640]{2,1,0:T(8,128)}) custom-call(s32[1]{0:T(128)} %bitcast.36.tab, bf16[1280,512]{1,0:T(8,128)(2,1)} %get-tuple-element.37.c_own, bf16[1280,512]{1,0:T(8,128)(2,1)} %get-tuple-element.38.c_oth, bf16[2,512,640]{2,1,0:T(8,128)(2,1)} %get-tuple-element.39.act_own, ...), custom_call_target="tpu_custom_call" | custom-call | flops 1677721600 | bytes 8388608 | tf_op jit(solution)/shard_map/grad_out_chunk/pallas_call | solution.py:203
  43.4 2.7 %collective-permute-start.21 = (f32[4,160,640]{2,1,0:T(8,128)}, f32[4,160,640]{2,1,0:T(8,128)S(1)}, u32[]{:S(2)}, u32[]{:S(2)}) collective-permute-start(f32[4,160,640]{2,1,0:T(8,128)} %get-tuple-element.44), channel_id=1, source_target_pairs={{0,4},{32,100},{8,12},{40,108},{16,20},{48,116},{24,28},{56,124},{... | collective-permute-start | bytes 4915208 | tf_op jit(solution)/shard_map/ppermute | solution.py:269
  46.1 6.0 %grad_out_chunk.2 = (f32[4,160,640]{2,1,0:T(8,128)}, f32[4,160,640]{2,1,0:T(8,128)}) custom-call(s32[1]{0:T(128)} %bitcast.34.tab, bf16[1280,512]{1,0:T(8,128)(2,1)} %get-tuple-element.37.c_own, bf16[1280,512]{1,0:T(8,128)(2,1)} %get-tuple-element.38.c_oth, bf16[2,512,640]{2,1,0:T(8,128)(2,1)} %get-tuple-element.39.act_own, ...), custom_call_target="tpu_custom_call" | custom-call | flops 1677721600 | bytes 8388608 | tf_op jit(solution)/shard_map/grad_out_chunk/pallas_call | solution.py:203
  53.0 9.1 %grad_in_chunk.3 = (f32[640,640]{1,0:T(8,128)}, f32[640,640]{1,0:T(8,128)}, f32[2,2,160,640]{3,2,1,0:T(8,128)}, f32[2,2,160,640]{3,2,1,0:T(8,128)}) custom-call(s32[5]{0:T(128)} %stack.90.tab, bf16[2,2,640,512]{3,2,1,0:T(8,128)(2,1)} %get-tuple-element.25.d_own, bf16[2,2,640,512]{3,2,1,0:T(8,128)(2,1)} %get-tuple-element.28.d_oth, bf16[512,1280]{1,0:T(8,128)(2,1)} %n_own.3, ...), custom_call_target="tpu_custom_call" | custom-call | flops 3355443200 | bytes 12582912 | tf_op jit(solution)/shard_map/grad_in_chunk/pallas_call | solution.py:157
  62.1 4.1 %collective-permute-start.3 = (f32[640,640]{1,0:T(8,128)}, f32[640,640]{1,0:T(8,128)}, u32[]{:S(2)}, u32[]{:S(2)}) collective-permute-start(f32[640,640]{1,0:T(8,128)} %get-tuple-element.32), channel_id=1, source_target_pairs={{0,8},{32,56},{8,0},{40,48},{16,24},{48,40},{24,16},{56,32},{1,9},... | collective-permute-start | bytes 4915208 | tf_op jit(solution)/shard_map/ppermute | solution.py:269
  66.9 9.2 %grad_in_chunk.2 = (f32[640,640]{1,0:T(8,128)}, f32[640,640]{1,0:T(8,128)}, f32[2,2,160,640]{3,2,1,0:T(8,128)}, f32[2,2,160,640]{3,2,1,0:T(8,128)}) custom-call(s32[5]{0:T(128)} %stack.87.tab, bf16[2,2,640,512]{3,2,1,0:T(8,128)(2,1)} %get-tuple-element.25.d_own, bf16[2,2,640,512]{3,2,1,0:T(8,128)(2,1)} %get-tuple-element.28.d_oth, bf16[512,1280]{1,0:T(8,128)(2,1)} %n_own.3, ...), custom_call_target="tpu_custom_call" | custom-call | flops 3355443200 | bytes 12582912 | tf_op jit(solution)/shard_map/grad_in_chunk/pallas_call | solution.py:157
  76.3 8.1 %back.2 = f32[512,1280]{1,0:T(8,128)} custom-call(s32[1]{0:T(128)} %bitcast.5.core_ref, bf16[2,512,1280]{2,1,0:T(8,128)(2,1)} %get-tuple-element.46.d_ref, bf16[2,2,2,640,1280]{4,3,2,1,0:T(8,128)(2,1)} %bitcast.99), custom_call_target="tpu_custom_call" | custom-call | flops 3355443200 | bytes 12582912 | tf_op jit(solution)/shard_map/back/pallas_call | solution.py:246
  84.4 2.8 %collective-permute-start.10 = (f32[2,2,160,640]{3,2,1,0:T(8,128)}, f32[2,2,160,640]{3,2,1,0:T(8,128)S(1)}, u32[]{:S(2)}, u32[]{:S(2)}) collective-permute-start(f32[2,2,160,640]{3,2,1,0:T(8,128)} %get-tuple-element.36), channel_id=1, source_target_pairs={{0,1},{32,35},{8,9},{40,43},{16,17},{48,51},{24,25},{56,59},{1,0},... | collective-permute-start | bytes 4915208 | tf_op jit(solution)/shard_map/ppermute | solution.py:269
  87.4 1.3 copy-done.15
  89.1 1.7 add_bitcast_fusion.1
  90.8 1.5 fusion.1
  92.6 0.9 copy-done.13
  93.4 1.8 add_bitcast_fusion.4
  95.2 7.7 %collective-permute-done.2 = f32[640,640]{1,0:T(8,128)} collective-permute-done((f32[640,640]{1,0:T(8,128)}, f32[640,640]{1,0:T(8,128)}, u32[]{:S(2)}, u32[]{:S(2)}) %collective-permute-start.2) | collective-permute-done | bytes 1638432 | tf_op jit(solution)/shard_map/ppermute | solution.py:269
  102.9 1.6 add_bitcast_fusion.5
  104.6 1.4 fusion.11
  106.3 0.8 copy-done.11
  107.4 16.5 %collective-permute-done.9 = f32[2,2,160,640]{3,2,1,0:T(8,128)S(1)} collective-permute-done((f32[2,2,160,640]{3,2,1,0:T(8,128)S(1)}, f32[2,2,160,640]{3,2,1,0:T(8,128)S(1)}, u32[]{:S(2)}, u32[]{:S(2)}) %collective-permute-start.9) | collective-permute-done | bytes 1638432 | tf_op jit(solution)/shard_map/ppermute | solution.py:269
  124.0 1.4 fusion.6
  125.7 2.2 %fusion.4 = f32[4,160,640]{2,1,0:T(8,128)S(1)} fusion(f32[4,160,640]{2,1,0:T(8,128)} %collective-permute-done.22, s32[]{:T(128)S(6)} %select_n.367, f32[1,4,160,640]{3,2,1,0:T(8,128)} %copy-done.6, f32[1,4,160,640]{3,2,1,0:T(8,128)S(1)} %add_bitcast_fusion), kind=kLoop, calls=%fused_computation.16 | loop fusion | flops 819200 | bytes 6553604 | tf_op jit(solution)/shard_map/add | solution.py:289
  128.1 2.6 %collective-permute-start.23 = (f32[2,4,40,640]{3,2,1,0:T(8,128)S(1)}, f32[2,4,40,640]{3,2,1,0:T(8,128)S(1)}, u32[]{:S(2)}, u32[]{:S(2)}) collective-permute-start(f32[2,4,40,640]{3,2,1,0:T(8,128)S(1)} %pad_maximum_fusion.2), channel_id=1, source_target_pairs={{0,8},{32,56},{8,0},{40,48},{16,24},{48,40},{24,16},{56,32},{1,9},... | collective-permute-start | bytes 2457608 | tf_op jit(solution)/shard_map/ppermute | solution.py:269
  130.7 1.8 fusion.14
  132.7 2.7 %collective-permute-start.5 = (f32[2,4,40,640]{3,2,1,0:T(8,128)S(1)}, f32[2,4,40,640]{3,2,1,0:T(8,128)S(1)}, u32[]{:S(2)}, u32[]{:S(2)}) collective-permute-start(f32[2,4,40,640]{3,2,1,0:T(8,128)S(1)} %pad_maximum_fusion), channel_id=1, source_target_pairs={{0,1},{32,35},{8,9},{40,43},{16,17},{48,51},{24,25},{56,59},{1,0},... | collective-permute-start | bytes 2457608 | tf_op jit(solution)/shard_map/ppermute | solution.py:269
  135.5 19.0 %collective-permute-done.11 = f32[2,2,160,640]{3,2,1,0:T(8,128)} collective-permute-done((f32[2,2,160,640]{3,2,1,0:T(8,128)}, f32[2,2,160,640]{3,2,1,0:T(8,128)}, u32[]{:S(2)}, u32[]{:S(2)}) %collective-permute-start.11) | collective-permute-done | bytes 1638432 | tf_op jit(solution)/shard_map/ppermute | solution.py:269
  154.4 1.6 fusion.9
  156.3 3.3 %collective-permute-start.12 = (f32[2,2,2,40,640]{4,3,2,1,0:T(8,128)S(1)}, f32[2,2,2,40,640]{4,3,2,1,0:T(8,128)S(1)}, u32[]{:S(2)}, u32[]{:S(2)}) collective-permute-start(f32[2,2,2,40,640]{4,3,2,1,0:T(8,128)S(1)} %pad_maximum_fusion.1), channel_id=1, source_target_pairs={{0,4},{32,100},{8,12},{40,108},{16,20},{48,116},{24,28},{56,124},{... | collective-permute-start | bytes 2457608 | tf_op jit(solution)/shard_map/ppermute | solution.py:269
  159.6 8.4 %back.3 = bf16[512,1280]{1,0:T(8,128)(2,1)} custom-call(s32[1]{0:T(128)} %bitcast.5.core_ref, bf16[2,512,1280]{2,1,0:T(8,128)(2,1)} %get-tuple-element.45.d_ref, bf16[2,2,2,640,1280]{4,3,2,1,0:T(8,128)(2,1)} %bitcast.100, f32[512,1280]{1,0:T(8,128)} %collective-permute-done.29.rest_0_), custom_call_target="tpu_custom_call" | custom-call | flops 3355443200 | bytes 12582912 | tf_op jit(solution)/shard_map/back/pallas_call | solution.py:246
  168.6 0.7 collective-permute-done.12
  169.6 5.7 %collective-permute-done.24 = f32[4,40,640]{2,1,0:T(8,128)S(1)} collective-permute-done((f32[4,40,640]{2,1,0:T(8,128)S(1)}, f32[4,40,640]{2,1,0:T(8,128)S(1)}, u32[]{:S(2)}, u32[]{:S(2)}) %collective-permute-start.24) | collective-permute-done | bytes 409632 | tf_op jit(solution)/shard_map/ppermute | solution.py:269
  175.4 2.9 %collective-permute-start.25 = (f32[2,40,640]{2,1,0:T(8,128)S(1)}, f32[2,40,640]{2,1,0:T(8,128)S(1)}, u32[]{:S(2)}, u32[]{:S(2)}) collective-permute-start(f32[2,40,640]{2,1,0:T(8,128)S(1)} %pad_maximum_fusion.6), channel_id=1, source_target_pairs={{0,1},{32,35},{8,9},{40,43},{16,17},{48,51},{24,25},{56,59},{1,0},... | collective-permute-start | bytes 614408 | tf_op jit(solution)/shard_map/ppermute | solution.py:269
  178.9 2.6 %collective-permute-start.14 = (f32[2,40,640]{2,1,0:T(8,128)S(1)}, f32[2,40,640]{2,1,0:T(8,128)S(1)}, u32[]{:S(2)}, u32[]{:S(2)}) collective-permute-start(f32[2,40,640]{2,1,0:T(8,128)S(1)} %pad_maximum_fusion.5), channel_id=1, source_target_pairs={{0,8},{32,56},{8,0},{40,48},{16,24},{48,40},{24,16},{56,32},{1,9},... | collective-permute-start | bytes 614408 | tf_op jit(solution)/shard_map/ppermute | solution.py:269
  182.2 2.8 %collective-permute-done.7 = f32[2,40,640]{2,1,0:T(8,128)S(1)} collective-permute-done((f32[2,40,640]{2,1,0:T(8,128)S(1)}, f32[2,40,640]{2,1,0:T(8,128)S(1)}, u32[]{:S(2)}, u32[]{:S(2)}) %collective-permute-start.7) | collective-permute-done | bytes 204832 | tf_op jit(solution)/shard_map/ppermute | solution.py:269
  185.3 3.6 %collective-permute-done.8 = f32[40,640]{1,0:T(8,128)S(1)} collective-permute-done((f32[40,640]{1,0:T(8,128)S(1)}, f32[40,640]{1,0:T(8,128)S(1)}, u32[]{:S(2)}, u32[]{:S(2)}) %collective-permute-start.8) | collective-permute-done | bytes 102432 | tf_op jit(solution)/shard_map/ppermute | solution.py:269
  188.9 1.2 collective-permute-done.15
  190.2 3.3 %collective-permute-start.18 = (f32[40,1280]{1,0:T(8,128)S(1)}, f32[40,1280]{1,0:T(8,128)S(1)}, u32[]{:S(2)}, u32[]{:S(2)}) collective-permute-start(f32[40,1280]{1,0:T(8,128)S(1)} %maximum_multiply_fusion.1), channel_id=1, source_target_pairs={{68,0},{76,8},{84,16},{92,24},{69,1},{77,9},{85,17},{93,25},{70,2}... | collective-permute-start | bytes 614408 | tf_op jit(solution)/shard_map/ppermute | solution.py:269
  194.2 4.9 %collective-permute-start.16 = (f32[40,1280]{1,0:T(8,128)S(1)}, f32[40,1280]{1,0:T(8,128)S(1)}, u32[]{:S(2)}, u32[]{:S(2)}) collective-permute-start(f32[40,1280]{1,0:T(8,128)S(1)} %maximum_multiply_fusion.1), channel_id=1, source_target_pairs={{4,0},{12,8},{20,16},{28,24},{5,1},{13,9},{21,17},{29,25},{6,2},{1... | collective-permute-start | bytes 614408 | tf_op jit(solution)/shard_map/ppermute | solution.py:269
  199.3 5.0 %collective-permute-done.27 = f32[40,640]{1,0:T(8,128)S(1)} collective-permute-done((f32[40,640]{1,0:T(8,128)S(1)}, f32[40,640]{1,0:T(8,128)S(1)}, u32[]{:S(2)}, u32[]{:S(2)}) %collective-permute-start.27) | collective-permute-done | bytes 102432 | tf_op jit(solution)/shard_map/ppermute | solution.py:269
  204.4 7.2 %collective-permute-start.28 = (f32[2,40,640]{2,1,0:T(8,128)S(1)}, f32[2,40,640]{2,1,0:T(8,128)S(1)}, u32[]{:S(2)}, u32[]{:S(2)}) collective-permute-start(f32[2,40,640]{2,1,0:T(8,128)S(1)} %fusion.17), channel_id=1, source_target_pairs={{0,32},{32,0},{8,40},{40,8},{16,48},{48,16},{24,56},{56,24},{1,33}... | collective-permute-start | bytes 614408 | tf_op jit(solution)/shard_map/ppermute | solution.py:269
  211.9 0.7 collective-permute-done.28
  212.8 0.8 pad_maximum_fusion.3
  213.5 0.7 collective-permute-done.19
  214.3 1.0 broadcast_select_fusion
  (114 shorter events, 7.8 us)
Async XLA Ops:
  0.6 3.2 %copy-start.7 = (bf16[512,1280]{1,0:T(8,128)(2,1)S(1)}, bf16[512,1280]{1,0:T(8,128)(2,1)}, u32[]{:S(2)}) copy-start(bf16[512,1280]{1,0:T(8,128)(2,1)} %n_own.3) | copy-start | bytes 3932164
  5.6 15.5 %collective-permute-start = (f32[512,1280]{1,0:T(8,128)}, f32[512,1280]{1,0:T(8,128)S(1)}, u32[]{:S(2)}, u32[]{:S(2)}) collective-permute-start(f32[512,1280]{1,0:T(8,128)} %convert_element_type.6), channel_id=1, source_target_pairs={{0,32},{32,0},{8,40},{40,8},{16,48},{48,16},{24,56},{56,24},{1,33}... | collective-permute-start | bytes 7864328 | tf_op jit(solution)/shard_map/ppermute | solution.py:269
  7.0 14.1 %collective-permute-start.1 = (f32[512,1280]{1,0:T(8,128)}, f32[512,1280]{1,0:T(8,128)}, u32[]{:S(2)}, u32[]{:S(2)}) collective-permute-start(f32[512,1280]{1,0:T(8,128)} %convert_element_type.7), channel_id=1, source_target_pairs={{0,32},{32,0},{8,40},{40,8},{16,48},{48,16},{24,56},{56,24},{1,33}... | collective-permute-start | bytes 7864328 | tf_op jit(solution)/shard_map/ppermute | solution.py:269
  21.0 1.5 copy-start.8
  43.4 40.9 %collective-permute-start.21 = (f32[4,160,640]{2,1,0:T(8,128)}, f32[4,160,640]{2,1,0:T(8,128)S(1)}, u32[]{:S(2)}, u32[]{:S(2)}) collective-permute-start(f32[4,160,640]{2,1,0:T(8,128)} %get-tuple-element.44), channel_id=1, source_target_pairs={{0,4},{32,100},{8,12},{40,108},{16,20},{48,116},{24,28},{56,124},{... | collective-permute-start | bytes 4915208 | tf_op jit(solution)/shard_map/ppermute | solution.py:269
  52.1 35.3 %collective-permute-start.20 = (f32[4,160,640]{2,1,0:T(8,128)}, f32[4,160,640]{2,1,0:T(8,128)}, u32[]{:S(2)}, u32[]{:S(2)}) collective-permute-start(f32[4,160,640]{2,1,0:T(8,128)} %get-tuple-element.42), channel_id=1, source_target_pairs={{0,4},{32,100},{8,12},{40,108},{16,20},{48,116},{24,28},{56,124},{... | collective-permute-start | bytes 4915208 | tf_op jit(solution)/shard_map/ppermute | solution.py:269
  62.1 30.5 %collective-permute-start.3 = (f32[640,640]{1,0:T(8,128)}, f32[640,640]{1,0:T(8,128)}, u32[]{:S(2)}, u32[]{:S(2)}) collective-permute-start(f32[640,640]{1,0:T(8,128)} %get-tuple-element.32), channel_id=1, source_target_pairs={{0,8},{32,56},{8,0},{40,48},{16,24},{48,40},{24,16},{56,32},{1,9},... | collective-permute-start | bytes 4915208 | tf_op jit(solution)/shard_map/ppermute | solution.py:269
  76.1 26.8 %collective-permute-start.2 = (f32[640,640]{1,0:T(8,128)}, f32[640,640]{1,0:T(8,128)}, u32[]{:S(2)}, u32[]{:S(2)}) collective-permute-start(f32[640,640]{1,0:T(8,128)} %get-tuple-element.30), channel_id=1, source_target_pairs={{0,8},{32,56},{8,0},{40,48},{16,24},{48,40},{24,16},{56,32},{1,9},... | collective-permute-start | bytes 4915208 | tf_op jit(solution)/shard_map/ppermute | solution.py:269
  76.3 10.9 %copy-start.10 = (f32[4,160,640]{2,1,0:T(8,128)S(1)}, f32[4,160,640]{2,1,0:T(8,128)}, u32[]{:S(2)}) copy-start(f32[4,160,640]{2,1,0:T(8,128)} %get-tuple-element.43) | copy-start | bytes 4915204
  84.4 75.2 %collective-permute-start.29 = (f32[512,1280]{1,0:T(8,128)}, f32[512,1280]{1,0:T(8,128)}, u32[]{:S(2)}, u32[]{:S(2)}) collective-permute-start(f32[512,1280]{1,0:T(8,128)} %back.2), channel_id=1, source_target_pairs={{0,32},{32,0},{8,40},{40,8},{16,48},{48,16},{24,56},{56,24},{1,33}... | collective-permute-start | bytes 7864328 | tf_op jit(solution)/shard_map/ppermute | solution.py:269
  84.4 21.9 %collective-permute-start.10 = (f32[2,2,160,640]{3,2,1,0:T(8,128)}, f32[2,2,160,640]{3,2,1,0:T(8,128)S(1)}, u32[]{:S(2)}, u32[]{:S(2)}) collective-permute-start(f32[2,2,160,640]{3,2,1,0:T(8,128)} %get-tuple-element.36), channel_id=1, source_target_pairs={{0,1},{32,35},{8,9},{40,43},{16,17},{48,51},{24,25},{56,59},{1,0},... | collective-permute-start | bytes 4915208 | tf_op jit(solution)/shard_map/ppermute | solution.py:269
  87.2 1.4 copy-start.15
  87.2 1.9 copy-start.9
  88.6 35.2 %collective-permute-start.9 = (f32[2,2,160,640]{3,2,1,0:T(8,128)S(1)}, f32[2,2,160,640]{3,2,1,0:T(8,128)S(1)}, u32[]{:S(2)}, u32[]{:S(2)}) collective-permute-start(f32[2,2,160,640]{3,2,1,0:T(8,128)S(1)} %copy-done.15), channel_id=1, source_target_pairs={{0,1},{32,35},{8,9},{40,43},{16,17},{48,51},{24,25},{56,59},{1,0},... | collective-permute-start | bytes 4915208 | tf_op jit(solution)/shard_map/ppermute | solution.py:269
  90.8 1.8 copy-start.6
  90.8 2.6 %copy-start.13 = (f32[640,640]{1,0:T(8,128)S(1)}, f32[640,640]{1,0:T(8,128)}, u32[]{:S(2)}) copy-start(f32[640,640]{1,0:T(8,128)} %get-tuple-element.31) | copy-start | bytes 4915204
  92.5 33.2 %collective-permute-start.22 = (f32[4,160,640]{2,1,0:T(8,128)}, f32[4,160,640]{2,1,0:T(8,128)}, u32[]{:S(2)}, u32[]{:S(2)}) collective-permute-start(f32[4,160,640]{2,1,0:T(8,128)} %fusion.1), channel_id=1, source_target_pairs={{0,68},{32,36},{8,76},{40,44},{16,84},{48,52},{24,92},{56,60},{1,6... | collective-permute-start | bytes 4915208 | tf_op jit(solution)/shard_map/ppermute | solution.py:269
  93.4 9.5 %copy-start.14 = (f32[640,640]{1,0:T(8,128)S(1)}, f32[640,640]{1,0:T(8,128)}, u32[]{:S(2)}) copy-start(f32[640,640]{1,0:T(8,128)} %get-tuple-element.29) | copy-start | bytes 4915204
  95.2 9.3 %copy-start = (f32[1,640,640]{2,1,0:T(8,128)}, f32[1,640,640]{2,1,0:T(8,128)S(1)}, u32[]{:S(2)}) copy-start(f32[1,640,640]{2,1,0:T(8,128)S(1)} %add_bitcast_fusion.4) | copy-start | bytes 4915204
  104.5 1.8 copy-start.2
  104.5 2.6 %copy-start.11 = (f32[2,2,160,640]{3,2,1,0:T(8,128)S(1)}, f32[2,2,160,640]{3,2,1,0:T(8,128)}, u32[]{:S(2)}) copy-start(f32[2,2,160,640]{3,2,1,0:T(8,128)} %get-tuple-element.35) | copy-start | bytes 4915204
  106.3 24.4 %collective-permute-start.4 = (f32[640,640]{1,0:T(8,128)}, f32[640,640]{1,0:T(8,128)}, u32[]{:S(2)}, u32[]{:S(2)}) collective-permute-start(f32[640,640]{1,0:T(8,128)} %fusion.11), channel_id=1, source_target_pairs={{0,24},{32,40},{8,16},{40,32},{16,8},{48,56},{24,0},{56,48},{1,25}... | collective-permute-start | bytes 4915208 | tf_op jit(solution)/shard_map/ppermute | solution.py:269
  107.2 16.7 %copy-start.12 = (f32[2,2,160,640]{3,2,1,0:T(8,128)S(1)}, f32[2,2,160,640]{3,2,1,0:T(8,128)}, u32[]{:S(2)}) copy-start(f32[2,2,160,640]{3,2,1,0:T(8,128)} %get-tuple-element.33) | copy-start | bytes 4915204
  124.0 1.7 copy-start.4
  125.7 28.7 %collective-permute-start.11 = (f32[2,2,160,640]{3,2,1,0:T(8,128)}, f32[2,2,160,640]{3,2,1,0:T(8,128)}, u32[]{:S(2)}, u32[]{:S(2)}) collective-permute-start(f32[2,2,160,640]{3,2,1,0:T(8,128)} %fusion.6), channel_id=1, source_target_pairs={{0,3},{32,33},{8,11},{40,41},{16,19},{48,49},{24,27},{56,57},{1,2}... | collective-permute-start | bytes 4915208 | tf_op jit(solution)/shard_map/ppermute | solution.py:269
  127.9 2.8 %copy-start.3 = (f32[1,640,640]{2,1,0:T(8,128)S(1)}, f32[1,640,640]{2,1,0:T(8,128)}, u32[]{:S(2)}) copy-start(f32[1,640,640]{2,1,0:T(8,128)} %copy-done.2) | copy-start | bytes 4915204
  128.0 2.7 %copy-start.1 = (f32[1,640,640]{2,1,0:T(8,128)S(1)}, f32[1,640,640]{2,1,0:T(8,128)}, u32[]{:S(2)}) copy-start(f32[1,640,640]{2,1,0:T(8,128)} %copy-done) | copy-start | bytes 4915204
  128.1 39.9 %collective-permute-start.23 = (f32[2,4,40,640]{3,2,1,0:T(8,128)S(1)}, f32[2,4,40,640]{3,2,1,0:T(8,128)S(1)}, u32[]{:S(2)}, u32[]{:S(2)}) collective-permute-start(f32[2,4,40,640]{3,2,1,0:T(8,128)S(1)} %pad_maximum_fusion.2), channel_id=1, source_target_pairs={{0,8},{32,56},{8,0},{40,48},{16,24},{48,40},{24,16},{56,32},{1,9},... | collective-permute-start | bytes 2457608 | tf_op jit(solution)/shard_map/ppermute | solution.py:269
  132.7 21.8 %copy-start.5 = (f32[1,2,2,160,640]{4,3,2,1,0:T(8,128)S(1)}, f32[1,2,2,160,640]{4,3,2,1,0:T(8,128)}, u32[]{:S(2)}) copy-start(f32[1,2,2,160,640]{4,3,2,1,0:T(8,128)} %copy-done.4) | copy-start | bytes 4915204
  132.7 35.5 %collective-permute-start.5 = (f32[2,4,40,640]{3,2,1,0:T(8,128)S(1)}, f32[2,4,40,640]{3,2,1,0:T(8,128)S(1)}, u32[]{:S(2)}, u32[]{:S(2)}) collective-permute-start(f32[2,4,40,640]{3,2,1,0:T(8,128)S(1)} %pad_maximum_fusion), channel_id=1, source_target_pairs={{0,1},{32,35},{8,9},{40,43},{16,17},{48,51},{24,25},{56,59},{1,0},... | collective-permute-start | bytes 2457608 | tf_op jit(solution)/shard_map/ppermute | solution.py:269
  156.3 13.0 %collective-permute-start.12 = (f32[2,2,2,40,640]{4,3,2,1,0:T(8,128)S(1)}, f32[2,2,2,40,640]{4,3,2,1,0:T(8,128)S(1)}, u32[]{:S(2)}, u32[]{:S(2)}) collective-permute-start(f32[2,2,2,40,640]{4,3,2,1,0:T(8,128)S(1)} %pad_maximum_fusion.1), channel_id=1, source_target_pairs={{0,4},{32,100},{8,12},{40,108},{16,20},{48,116},{24,28},{56,124},{... | collective-permute-start | bytes 2457608 | tf_op jit(solution)/shard_map/ppermute | solution.py:269
  168.1 7.2 %collective-permute-start.24 = (f32[4,40,640]{2,1,0:T(8,128)S(1)}, f32[4,40,640]{2,1,0:T(8,128)S(1)}, u32[]{:S(2)}, u32[]{:S(2)}) collective-permute-start(f32[4,40,640]{2,1,0:T(8,128)S(1)} %dynamic-slice_bitcast_fusion), channel_id=1, source_target_pairs={{0,24},{32,40},{8,16},{40,32},{16,8},{48,56},{24,0},{56,48},{1,25}... | collective-permute-start | bytes 1228808 | tf_op jit(solution)/shard_map/ppermute | solution.py:269
  168.4 10.0 %collective-permute-start.6 = (f32[4,40,640]{2,1,0:T(8,128)S(1)}, f32[4,40,640]{2,1,0:T(8,128)S(1)}, u32[]{:S(2)}, u32[]{:S(2)}) collective-permute-start(f32[4,40,640]{2,1,0:T(8,128)S(1)} %dynamic-slice_bitcast_fusion.2), channel_id=1, source_target_pairs={{0,3},{32,33},{8,11},{40,41},{16,19},{48,49},{24,27},{56,57},{1,2}... | collective-permute-start | bytes 1228808 | tf_op jit(solution)/shard_map/ppermute | solution.py:269
  169.5 9.2 %collective-permute-start.13 = (f32[2,2,40,640]{3,2,1,0:T(8,128)S(1)}, f32[2,2,40,640]{3,2,1,0:T(8,128)S(1)}, u32[]{:S(2)}, u32[]{:S(2)}) collective-permute-start(f32[2,2,40,640]{3,2,1,0:T(8,128)S(1)} %dynamic-slice_bitcast_fusion.1), channel_id=1, source_target_pairs={{0,68},{32,36},{8,76},{40,44},{16,84},{48,52},{24,92},{56,60},{1,6... | collective-permute-start | bytes 1228808 | tf_op jit(solution)/shard_map/ppermute | solution.py:269
  175.4 6.6 %collective-permute-start.25 = (f32[2,40,640]{2,1,0:T(8,128)S(1)}, f32[2,40,640]{2,1,0:T(8,128)S(1)}, u32[]{:S(2)}, u32[]{:S(2)}) collective-permute-start(f32[2,40,640]{2,1,0:T(8,128)S(1)} %pad_maximum_fusion.6), channel_id=1, source_target_pairs={{0,1},{32,35},{8,9},{40,43},{16,17},{48,51},{24,25},{56,59},{1,0},... | collective-permute-start | bytes 614408 | tf_op jit(solution)/shard_map/ppermute | solution.py:269
  178.4 6.5 %collective-permute-start.7 = (f32[2,40,640]{2,1,0:T(8,128)S(1)}, f32[2,40,640]{2,1,0:T(8,128)S(1)}, u32[]{:S(2)}, u32[]{:S(2)}) collective-permute-start(f32[2,40,640]{2,1,0:T(8,128)S(1)} %pad_maximum_fusion.4), channel_id=1, source_target_pairs={{0,4},{32,100},{8,12},{40,108},{16,20},{48,116},{24,28},{56,124},{... | collective-permute-start | bytes 614408 | tf_op jit(solution)/shard_map/ppermute | solution.py:269
  178.9 6.3 %collective-permute-start.14 = (f32[2,40,640]{2,1,0:T(8,128)S(1)}, f32[2,40,640]{2,1,0:T(8,128)S(1)}, u32[]{:S(2)}, u32[]{:S(2)}) collective-permute-start(f32[2,40,640]{2,1,0:T(8,128)S(1)} %pad_maximum_fusion.5), channel_id=1, source_target_pairs={{0,8},{32,56},{8,0},{40,48},{16,24},{48,40},{24,16},{56,32},{1,9},... | collective-permute-start | bytes 614408 | tf_op jit(solution)/shard_map/ppermute | solution.py:269
  182.1 17.0 %collective-permute-start.26 = (f32[40,640]{1,0:T(8,128)S(1)}, f32[40,640]{1,0:T(8,128)S(1)}, u32[]{:S(2)}, u32[]{:S(2)}) collective-permute-start(f32[40,640]{1,0:T(8,128)S(1)} %dynamic-slice_bitcast_fusion.3), channel_id=1, source_target_pairs={{0,3},{32,33},{8,11},{40,41},{16,19},{48,49},{24,27},{56,57},{1,2}... | collective-permute-start | bytes 307208 | tf_op jit(solution)/shard_map/ppermute | solution.py:269
  185.0 3.9 %collective-permute-start.8 = (f32[40,640]{1,0:T(8,128)S(1)}, f32[40,640]{1,0:T(8,128)S(1)}, u32[]{:S(2)}, u32[]{:S(2)}) collective-permute-start(f32[40,640]{1,0:T(8,128)S(1)} %dynamic-slice_bitcast_fusion.5), channel_id=1, source_target_pairs={{0,68},{32,36},{8,76},{40,44},{16,84},{48,52},{24,92},{56,60},{1,6... | collective-permute-start | bytes 307208 | tf_op jit(solution)/shard_map/ppermute | solution.py:269
  185.2 5.0 %collective-permute-start.15 = (f32[40,640]{1,0:T(8,128)S(1)}, f32[40,640]{1,0:T(8,128)S(1)}, u32[]{:S(2)}, u32[]{:S(2)}) collective-permute-start(f32[40,640]{1,0:T(8,128)S(1)} %dynamic-slice_bitcast_fusion.4), channel_id=1, source_target_pairs={{0,24},{32,40},{8,16},{40,32},{16,8},{48,56},{24,0},{56,48},{1,25}... | collective-permute-start | bytes 307208 | tf_op jit(solution)/shard_map/ppermute | solution.py:269
  190.2 21.4 %collective-permute-start.18 = (f32[40,1280]{1,0:T(8,128)S(1)}, f32[40,1280]{1,0:T(8,128)S(1)}, u32[]{:S(2)}, u32[]{:S(2)}) collective-permute-start(f32[40,1280]{1,0:T(8,128)S(1)} %maximum_multiply_fusion.1), channel_id=1, source_target_pairs={{68,0},{76,8},{84,16},{92,24},{69,1},{77,9},{85,17},{93,25},{70,2}... | collective-permute-start | bytes 614408 | tf_op jit(solution)/shard_map/ppermute | solution.py:269
  193.5 18.1 %collective-permute-start.17 = (f32[40,1280]{1,0:T(8,128)S(1)}, f32[40,1280]{1,0:T(8,128)S(1)}, u32[]{:S(2)}, u32[]{:S(2)}) collective-permute-start(f32[40,1280]{1,0:T(8,128)S(1)} %maximum_multiply_fusion.1), channel_id=1, source_target_pairs={{64,0},{72,8},{80,16},{88,24},{65,1},{73,9},{81,17},{89,25},{66,2}... | collective-permute-start | bytes 614408 | tf_op jit(solution)/shard_map/ppermute | solution.py:269
  194.2 17.4 %collective-permute-start.16 = (f32[40,1280]{1,0:T(8,128)S(1)}, f32[40,1280]{1,0:T(8,128)S(1)}, u32[]{:S(2)}, u32[]{:S(2)}) collective-permute-start(f32[40,1280]{1,0:T(8,128)S(1)} %maximum_multiply_fusion.1), channel_id=1, source_target_pairs={{4,0},{12,8},{20,16},{28,24},{5,1},{13,9},{21,17},{29,25},{6,2},{1... | collective-permute-start | bytes 614408 | tf_op jit(solution)/shard_map/ppermute | solution.py:269
  199.2 5.2 %collective-permute-start.27 = (f32[40,640]{1,0:T(8,128)S(1)}, f32[40,640]{1,0:T(8,128)S(1)}, u32[]{:S(2)}, u32[]{:S(2)}) collective-permute-start(f32[40,640]{1,0:T(8,128)S(1)} %fusion.20), channel_id=1, source_target_pairs={{0,64},{32,96},{8,72},{40,104},{16,80},{48,112},{24,88},{56,120},{... | collective-permute-start | bytes 307208 | tf_op jit(solution)/shard_map/ppermute | solution.py:269
  204.4 8.3 %collective-permute-start.28 = (f32[2,40,640]{2,1,0:T(8,128)S(1)}, f32[2,40,640]{2,1,0:T(8,128)S(1)}, u32[]{:S(2)}, u32[]{:S(2)}) collective-permute-start(f32[2,40,640]{2,1,0:T(8,128)S(1)} %fusion.17), channel_id=1, source_target_pairs={{0,32},{32,0},{8,40},{40,8},{16,48},{48,16},{24,56},{56,24},{1,33}... | collective-permute-start | bytes 614408 | tf_op jit(solution)/shard_map/ppermute | solution.py:269
  211.8 2.4 %collective-permute-start.19 = (f32[160,1280]{1,0:T(8,128)S(1)}, f32[160,1280]{1,0:T(8,128)S(1)}, u32[]{:S(2)}, u32[]{:S(2)}) collective-permute-start(f32[160,1280]{1,0:T(8,128)S(1)} %bitcast.104), channel_id=1, source_target_pairs={{0,32},{32,0},{8,40},{40,8},{16,48},{48,16},{24,56},{56,24},{1,33}... | collective-permute-start | bytes 2457608 | tf_op jit(solution)/shard_map/ppermute | solution.py:269
